TPU v7x, 512 devices: a whole 4x8x8 slice. The times are simulated.
512 devices in a mesh: pairs: 32 (over y, x), aux: 16 (over z, core).
Axes of the slice: x: 4, y: 8, z: 8, core: 2. Of those that a mesh axis runs over, the one named last changes fastest.
Arguments:
- factors: bfloat16 [4096, 2048, 128], P('aux', 'pairs'), may hold values from -1 to 1
- coefficients: bfloat16 [2048, 256, 128], P(('pairs', 'aux')), may hold values from -0.375 to 0.375
- amplitudes: bfloat16 [2048, 128, 128], P(('pairs', 'aux')), may hold values from -6 to 6
- domains: int32 [2048, 256], P(('pairs', 'aux')), may hold values from 0 to 4413, as said below
- partners: int32 [2048, 12], P(('pairs', 'aux')), may hold values from 0 to 2047, as said below
- couplings: float32 [2048, 12], P(('pairs', 'aux')), may hold values from -4 to 4
- energies: float32 [2048, 128], P(('pairs', 'aux')), may hold values from 0.5 to 4
Outputs:
- residual: float32 [2048, 128, 128], P(('pairs', 'aux'))
Inputs may be any that keep to these rules, and one draw needn't show every extreme that they name: `partners`: row p names 12 different pairs other than p, all within the run of 65 consecutive pair numbers centred on p, moved inward where it would pass 0 or 2047. `domains`: each row holds 256 different function numbers.
All inputs are finite; a program needn't handle non-finite values.
Results may differ from a plain program's by a relative error of at most 0.0065.
Values may be sent and summed in bfloat16 or wider, within the bound.
A program may use at most 128 MiB of HBM per device.

v0:
```python
import jax
import jax.numpy as jnp
from jax import lax
from jax.sharding import Mesh
from jax.sharding import PartitionSpec as P

AUX = ("aux_0", "aux_1")
PAIRS_AUX = ("pairs", "aux_0", "aux_1")


def summed_rows(shard, axes, dim):
    for axis in axes:
        shard = lax.psum_scatter(shard, axis, scatter_dimension=dim, tiled=True)
    return shard


def shortened(shard):
    return jax.tree.map(lambda a: a.astype(jnp.bfloat16) if a.dtype == jnp.float32 else a, shard)


def extended_2(cells, sides, width):
    for axis, dim in sides:
        count = lax.axis_size(axis)
        ends = count - 1
        head = lax.slice_in_dim(cells, 0, width, axis=dim)
        tail = lax.slice_in_dim(cells, cells.shape[dim] - width, cells.shape[dim], axis=dim)
        cells = jnp.concatenate(
            [
                lax.ppermute(tail, axis, [(i, (i + 1) % count) for i in range(ends)]),
                cells,
                lax.ppermute(head, axis, [((i + 1) % count, i) for i in range(ends)]),
            ],
            axis=dim,
        )
    return cells


def shards(factors, coefficients, amplitudes, domains, partners, couplings, energies):
    own_pairs = amplitudes.shape[0]
    dom_width = coefficients.shape[1]
    aux_count = lax.axis_size(AUX)
    group_size = own_pairs * aux_count
    reach_pairs = group_size // 2
    group_index = lax.axis_index("pairs")
    aux_index = lax.axis_index(AUX)
    partial_value = jnp.einsum("xpa,xpb->pab", factors, factors, preferred_element_type=jnp.float32)
    partial_value = lax.optimization_barrier(partial_value.astype(jnp.bfloat16)).astype(jnp.float32)
    exchange_k = summed_rows(partial_value.astype(jnp.bfloat16), AUX, 0).astype(jnp.float32)
    stacked = jnp.concatenate([coefficients, amplitudes], axis=1)
    extended = [
        extended_2(shortened(member), (("pairs", 0),), own_pairs).astype(member.dtype)
        for member in (stacked, domains)
    ]
    upper_half = aux_index >= aux_count // 2
    outgoing = tuple(
        (
            jnp.stack(
                [
                    member[own_pairs : 2 * own_pairs],
                    jnp.where(upper_half, member[:own_pairs], member[2 * own_pairs :]),
                ],
                axis=0,
            )
            for member in extended
        )
    )
    gathered = jax.tree.map(
        lambda part, own: part.astype(own.dtype),
        lax.all_gather(shortened(outgoing), AUX, axis=1, tiled=True),
        outgoing,
    )
    window_rows, window_funcs = [
        jnp.concatenate([member[1, reach_pairs:], member[0], member[1, :reach_pairs]], axis=0)
        for member in gathered
    ]
    first_pair = group_index * group_size - reach_pairs
    slots = partners - first_pair
    far_rows = window_rows[slots]
    far_funcs = window_funcs[slots]
    far_coeff = far_rows[:, :, :dom_width]
    far_amps = far_rows[:, :, dom_width:]
    matches = (domains[:, None, :, None] == far_funcs[:, :, None, :]).astype(jnp.bfloat16)
    matched = jnp.einsum(
        "pcfg,pcgn->pcfn", matches, far_coeff, preferred_element_type=jnp.float32
    ).astype(jnp.bfloat16)
    intersection = jnp.einsum(
        "pfa,pcfn->pcan", coefficients, matched, preferred_element_type=jnp.float32
    ).astype(jnp.bfloat16)
    mixed_rows = jnp.einsum(
        "pcan,pcnm->pcam", intersection, far_amps, preferred_element_type=jnp.float32
    ).astype(jnp.bfloat16)
    coupled = jnp.einsum(
        "pcam,pcbm->pcab", mixed_rows, intersection, preferred_element_type=jnp.float32
    )
    cycle_term = jnp.sum(couplings[:, :, None, None] * coupled, axis=1)
    diagonal_term = (energies[:, :, None] + energies[:, None, :]) * amplitudes.astype(jnp.float32)
    return exchange_k + diagonal_term - cycle_term


def solution(mesh):
    finer = Mesh(mesh.devices.reshape(mesh.shape["pairs"], 8, 2), ("pairs", "aux_0", "aux_1"))
    return jax.shard_map(
        shards,
        mesh=finer,
        in_specs=(
            P(AUX, "pairs", None),
            P(PAIRS_AUX, None, None),
            P(PAIRS_AUX, None, None),
            P(PAIRS_AUX, None),
            P(PAIRS_AUX, None),
            P(PAIRS_AUX, None),
            P(PAIRS_AUX, None),
        ),
        out_specs=P(PAIRS_AUX, None, None),
        check_vma=False,
    )
```

profile of v0, /device:TPU:1, one launch (start us, length us, event | category | flops | bytes accessed | tf_op | source)
XLA Modules:
  0.0 168.8 jit_solution(5495212050930020416)
XLA Ops:
  7.4 0.0 reduce-scatter.3.cloned.1.call-start
  7.4 10.2 %fusion.17 = bf16[64,128,128]{2,1,0:T(8,128)(2,1)} fusion(bf16[256,64,128]{2,1,0:T(8,128)(2,1)} %param.7), kind=kOutput, calls=%fused_computation.16 | convolution fusion | flops 537919488 | bytes 6291456 | tf_op jit(solution)/shard_map/xpa,xpb->pab/dot_general | solution.py:46
  17.6 0.0 reduce-scatter.3.cloned.1.call-update
  17.6 0.0 all-gather.2.cloned.1.call-start
  17.7 4.0 %collective-permute-start.2 = (bf16[4,384,128]{2,1,0:T(8,128)(2,1)S(1)}, bf16[4,384,128]{2,1,0:T(8,128)(2,1)S(1)}, u32[]{:S(2)}, u32[]{:S(2)}) collective-permute-start(bf16[4,384,128]{2,1,0:T(8,128)(2,1)S(1)} %constant_dynamic-update-slice_fusion), channel_id=1, source_target_pairs={{0,16},{16,32},{32,48},{48,64},{64,80},{80,96},{96,112},{112,128},... | collective-permute-start | bytes 1179656 | tf_op jit(solution)/shard_map/ppermute | solution.py:29
  21.7 1.3 collective-permute-start.3
  23.0 3.4 %collective-permute-done.2 = bf16[4,384,128]{2,1,0:T(8,128)(2,1)S(1)} collective-permute-done((bf16[4,384,128]{2,1,0:T(8,128)(2,1)S(1)}, bf16[4,384,128]{2,1,0:T(8,128)(2,1)S(1)}, u32[]{:S(2)}, u32[]{:S(2)}) %collective-permute-start.2) | collective-permute-done | bytes 393248 | tf_op jit(solution)/shard_map/ppermute | solution.py:29
  26.4 3.8 %collective-permute-done.3 = bf16[4,384,128]{2,1,0:T(8,128)(2,1)S(1)} collective-permute-done((bf16[4,384,128]{2,1,0:T(8,128)(2,1)S(1)}, bf16[4,384,128]{2,1,0:T(8,128)(2,1)S(1)}, u32[]{:S(2)}, u32[]{:S(2)}) %collective-permute-start.3) | collective-permute-done | bytes 393248 | tf_op jit(solution)/shard_map/ppermute | solution.py:31
  30.3 1.0 pad_maximum_fusion.1
  31.2 0.0 all-gather.2.cloned.1.call-update
  31.3 0.0 reduce-scatter.5.cloned.1.call-start
  31.3 6.1 %collective-permute-start = (s32[4,256]{1,0:T(4,128)S(1)}, s32[4,256]{1,0:T(4,128)S(1)}, u32[]{:S(2)}, u32[]{:S(2)}) collective-permute-start(s32[4,256]{1,0:T(4,128)S(1)} %copy-done.4), channel_id=1, source_target_pairs={{0,16},{16,32},{32,48},{48,64},{64,80},{80,96},{96,112},{112,128},... | collective-permute-start | bytes 12296 | tf_op jit(solution)/shard_map/ppermute | solution.py:29
  37.5 1.3 collective-permute-start.1
  38.8 0.1 reshape.7
  38.9 0.0 collective-permute-done
  38.9 3.3 %collective-permute-done.1 = s32[4,256]{1,0:T(4,128)S(1)} collective-permute-done((s32[4,256]{1,0:T(4,128)S(1)}, s32[4,256]{1,0:T(4,128)S(1)}, u32[]{:S(2)}, u32[]{:S(2)}) %collective-permute-start.1) | collective-permute-done | bytes 4128 | tf_op jit(solution)/shard_map/ppermute | solution.py:31
  42.2 26.7 %all_gather.6 = s32[2,64,256]{2,0,1:T(2,128)S(1)} all-gather(s32[2,4,256]{2,0,1:T(2,128)S(1)} %pad_add_fusion.1), channel_id=1, replica_groups=mesh['pairs'=32,'aux_0'=8,'aux_1'=2] {'aux_0','aux_1'}, dimensions={1}, use_global_device_ids=true | all-gather | bytes 139264 | tf_op jit(solution)/shard_map/all_gather | solution.py:69
  69.1 0.1 fusion.31
  69.2 0.6 gather_fusion
  69.8 10.4 %reduce-scatter.3.cloned.1.call-done = bf16[8,128,128]{2,1,0:T(8,128)(2,1)} async-done(((bf16[64,128,128]{2,1,0:T(8,128)(2,1)}), bf16[8,128,128]{2,1,0:T(8,128)(2,1)}) %reduce-scatter.3.cloned.1.call-update) | async-done | bytes 262160 | tf_op jit(solution)/shard_map/reduce_scatter | solution.py:13
  80.2 0.0 reduce-scatter.5.cloned.1.call-update
  80.2 46.0 %all-gather.2.cloned.1.call-done = bf16[2,64,384,128]{3,2,1,0:T(8,128)(2,1)} async-done(((bf16[2,4,384,128]{3,2,1,0:T(8,128)(2,1)}), bf16[2,64,384,128]{3,2,1,0:T(8,128)(2,1)}) %all-gather.2.cloned.1.call-update) | async-done | bytes 12582928 | tf_op jit(solution)/shard_map/all_gather | solution.py:69
  126.2 6.9 %slice_bitcast_fusion.2 = (bf16[32,384,128]{2,1,0:T(8,128)(2,1)}, bf16[32,384,128]{2,1,0:T(8,128)(2,1)}) fusion(bf16[2,64,384,128]{3,2,1,0:T(8,128)(2,1)} %all-gather.2.cloned.1.call-done), kind=kLoop, calls=%fused_computation.12 | loop fusion | bytes 12582912 | tf_op jit(solution)/shard_map/squeeze | solution.py:73
  133.2 1.8 %copy-done = bf16[2,64,384,128]{3,2,1,0:T(8,128)(2,1)S(1)} copy-done((bf16[2,64,384,128]{3,2,1,0:T(8,128)(2,1)S(1)}, bf16[2,64,384,128]{3,2,1,0:T(8,128)(2,1)}, u32[]{:S(2)}) %copy-start) | copy-done | bytes 12582936
  134.9 0.7 slice_bitcast_fusion
  135.7 8.4 %pad_maximum_fusion = bf16[128,384,128]{2,1,0:T(8,128)(2,1)} fusion(bf16[32,384,128]{2,1,0:T(8,128)(2,1)} %get-tuple-element.6, bf16[64,384,128]{2,1,0:T(8,128)(2,1)S(1)} %slice_bitcast_fusion, bf16[32,384,128]{2,1,0:T(8,128)(2,1)} %get-tuple-element.5), kind=kLoop, calls=%fused_computation.2 | loop fusion | flops 12582912 | bytes 25165824 | tf_op jit(solution)/shard_map/concatenate | solution.py:73
  144.1 8.0 %gather_fusion.1 = bf16[48,384,128]{2,1,0:T(8,128)(2,1)} fusion(bf16[128,384,128]{2,1,0:T(8,128)(2,1)} %pad_maximum_fusion, s32[1024]{0:T(1024)S(1)} %pad_clamp_fusion), kind=kCustom, calls=%fused_computation.1 | custom fusion | bytes 9437376 | tf_op jit(solution)/shard_map/gather | solution.py:78
  152.1 4.9 %fusion.20 = bf16[4,12,128,128]{3,2,1,0:T(8,128)(2,1)S(1)} fusion(bf16[4,12,384,128]{3,2,1,0:T(8,128)(2,1)} %bitcast.24, s32[4,12,256]{2,1,0:T(8,128)S(1)} %reshape.6, s32[4,256]{1,0:T(4,128)S(1)} %copy-done.4, bf16[4,256,128]{2,1,0:T(8,128)(2,1)S(1)} %copy-done.2), kind=kOutput, calls=%fused_computation.17 | convolution fusion | flops 1213464576 | bytes 5033984 | tf_op jit(solution)/shard_map/pfa,pcfn->pcan/dot_general | solution.py:86
  157.0 0.0 copy-start.3
  157.0 2.6 %multiply_reduce_fusion = f32[4,128,128]{2,1,0:T(8,128)S(1)} fusion(bf16[4,12,128,128]{3,2,1,0:T(8,128)(2,1)S(1)} %fusion.20, f32[4,12]{1,0:T(4,128)S(1)} %copy-done.6, bf16[4,12,384,128]{3,2,1,0:T(8,128)(2,1)} %bitcast.25), kind=kOutput, calls=%fused_computation.13 | convolution fusion | flops 404946944 | bytes 4982784 | tf_op jit(solution)/shard_map/pcam,pcbm->pcab/dot_general | solution.py:92
  159.6 0.0 reduce-scatter.5.cloned.1.call-done
  159.6 1.7 %add_subtract_fusion = f32[4,128,128]{2,1,0:T(8,128)} fusion(f32[4,128,128]{2,1,0:T(8,128)S(1)} %multiply_reduce_fusion, bf16[4,128,128]{2,1,0:T(8,128)(2,1)S(1)} %copy-done.1, bf16[4,128,128]{2,1,0:T(8,128)(2,1)} %reduce-scatter.5.cloned.1.call-done, f32[4,128]{1,0:T(4,128)S(1)} %copy-done.3), kind=kLoop, calls=%fused_computation.23 | loop fusion | flops 393216 | bytes 788480 | tf_op jit(solution)/shard_map/sub | solution.py:97
  (26 shorter events, 0.2 us)
Async XLA Ops:
  7.4 10.3 %copy-start.2 = (bf16[4,256,128]{2,1,0:T(8,128)(2,1)S(1)}, bf16[4,256,128]{2,1,0:T(8,128)(2,1)}, u32[]{:S(2)}) copy-start(bf16[4,256,128]{2,1,0:T(8,128)(2,1)} %param.8) | copy-start | bytes 786436
  7.4 10.3 %copy-start.1 = (bf16[4,128,128]{2,1,0:T(8,128)(2,1)S(1)}, bf16[4,128,128]{2,1,0:T(8,128)(2,1)}, u32[]{:S(2)}) copy-start(bf16[4,128,128]{2,1,0:T(8,128)(2,1)} %param.9) | copy-start | bytes 393220
  7.4 72.8 %reduce-scatter.3.cloned.1.call-start = ((), (), s32[]{:S(2)}) async-start(), calls=%async_computation.2 | async-start | bytes 2359296 | tf_op jit(solution)/shard_map/reduce_scatter | solution.py:13
  17.6 13.8 %copy-start.4 = (s32[4,256]{1,0:T(4,128)S(1)}, s32[4,256]{1,0:T(4,128)}, u32[]{:S(2)}) copy-start(s32[4,256]{1,0:T(4,128)} %param.10) | copy-start | bytes 12292
  17.6 21.2 %copy-start.5 = (s32[4,12]{1,0:T(4,128)S(1)}, s32[4,12]{1,0:T(4,128)}, u32[]{:S(2)}) copy-start(s32[4,12]{1,0:T(4,128)} %param.11) | copy-start | bytes 580
  17.6 108.6 %all-gather.2.cloned.1.call-start = ((), (), s32[]{:S(2)}) async-start(), calls=%async_computation.4 | async-start | bytes 13369344 | tf_op jit(solution)/shard_map/all_gather | solution.py:69
  17.7 8.7 %collective-permute-start.2 = (bf16[4,384,128]{2,1,0:T(8,128)(2,1)S(1)}, bf16[4,384,128]{2,1,0:T(8,128)(2,1)S(1)}, u32[]{:S(2)}, u32[]{:S(2)}) collective-permute-start(bf16[4,384,128]{2,1,0:T(8,128)(2,1)S(1)} %constant_dynamic-update-slice_fusion), channel_id=1, source_target_pairs={{0,16},{16,32},{32,48},{48,64},{64,80},{80,96},{96,112},{112,128},... | collective-permute-start | bytes 1179656 | tf_op jit(solution)/shard_map/ppermute | solution.py:29
  21.7 8.5 %collective-permute-start.3 = (bf16[4,384,128]{2,1,0:T(8,128)(2,1)S(1)}, bf16[4,384,128]{2,1,0:T(8,128)(2,1)S(1)}, u32[]{:S(2)}, u32[]{:S(2)}) collective-permute-start(bf16[4,384,128]{2,1,0:T(8,128)(2,1)S(1)} %constant_dynamic-update-slice_fusion), channel_id=1, source_target_pairs={{16,0},{32,16},{48,32},{64,48},{80,64},{96,80},{112,96},{128,112},... | collective-permute-start | bytes 1179656 | tf_op jit(solution)/shard_map/ppermute | solution.py:31
  31.3 128.3 %reduce-scatter.5.cloned.1.call-start = ((), (), s32[]{:S(2)}) async-start(), calls=%async_computation.3 | async-start | bytes 393216 | tf_op jit(solution)/shard_map/reduce_scatter | solution.py:13
  31.3 7.6 %collective-permute-start = (s32[4,256]{1,0:T(4,128)S(1)}, s32[4,256]{1,0:T(4,128)S(1)}, u32[]{:S(2)}, u32[]{:S(2)}) collective-permute-start(s32[4,256]{1,0:T(4,128)S(1)} %copy-done.4), channel_id=1, source_target_pairs={{0,16},{16,32},{32,48},{48,64},{64,80},{80,96},{96,112},{112,128},... | collective-permute-start | bytes 12296 | tf_op jit(solution)/shard_map/ppermute | solution.py:29
  37.5 4.8 %collective-permute-start.1 = (s32[4,256]{1,0:T(4,128)S(1)}, s32[4,256]{1,0:T(4,128)S(1)}, u32[]{:S(2)}, u32[]{:S(2)}) collective-permute-start(s32[4,256]{1,0:T(4,128)S(1)} %copy-done.4), channel_id=1, source_target_pairs={{16,0},{32,16},{48,32},{64,48},{80,64},{96,80},{112,96},{128,112},... | collective-permute-start | bytes 12296 | tf_op jit(solution)/shard_map/ppermute | solution.py:31
  126.2 8.7 %copy-start = (bf16[2,64,384,128]{3,2,1,0:T(8,128)(2,1)S(1)}, bf16[2,64,384,128]{3,2,1,0:T(8,128)(2,1)}, u32[]{:S(2)}) copy-start(bf16[2,64,384,128]{3,2,1,0:T(8,128)(2,1)} %all-gather.2.cloned.1.call-done) | copy-start | bytes 37748740
  152.1 4.9 %copy-start.6 = (f32[4,12]{1,0:T(4,128)S(1)}, f32[4,12]{1,0:T(4,128)}, u32[]{:S(2)}) copy-start(f32[4,12]{1,0:T(4,128)} %param.12) | copy-start | bytes 580
  157.0 2.6 %copy-start.3 = (f32[4,128]{1,0:T(4,128)S(1)}, f32[4,128]{1,0:T(4,128)}, u32[]{:S(2)}) copy-start(f32[4,128]{1,0:T(4,128)} %param.13) | copy-start | bytes 6148
Sparse Core Ops, SparseCore 0:
  17.7 62.4 reduce-scatter.2
  82.9 27.8 reduce-scatter.4
Sparse Core Ops, SparseCore 1:
  31.4 94.8 all-gather.1
where the time goes:
time: 169 us
  waiting for transfers between devices  67 us (40%)
  blocking collectives  26.7 us (16%)
  local copies, waits for them, and re-layouts  18.3 us (11%)
  matrix products  17.6 us (10%)
  between operations  15.1 us (9%)
  starting transfers between devices  12.8 us (8%)
  other arithmetic  11.2 us (7%)
    all_gather x1, waiting for transfers between devices, shards(): lax.all_gather(shortened(outgoing), AUX, axis=1, tiled=True)  46 us
    all_gather x1, blocking collectives, shards(): lax.all_gather(shortened(outgoing), AUX, axis=1, tiled=True)  26.7 us
    reduce_scatter x2, waiting for transfers between devices, summed_rows(): shard = lax.psum_scatter(shard, axis, scatter_dimension=dim, tiled=True)  10.4 us
    dot_general x1, matrix products, shards(): jnp.einsum('xpa,xpb->pab', factors, factors, preferred_element_type=jnp.f...  10.2 us
    ppermute x2, starting transfers between devices, extended_2(): lax.ppermute(tail, axis, [(i, (i + 1) % count) for i in range(ends)])  10.1 us
    concatenate x2, other arithmetic, shards(): jnp.concatenate([member[1, reach_pairs:], member[0], member[1, :reach_pai...  8.45 us
    gather x1, local copies, waits for them, and re-layouts, shards(): far_rows = window_rows[slots]  7.96 us
    ppermute x2, waiting for transfers between devices, extended_2(): lax.ppermute(head, axis, [((i + 1) % count, i) for i in range(ends)])  7.16 us
  transfers between devices with their start and end apart: 7, of which 5 were waited for; matrix products, arithmetic and copies ran while one was open for 20% of the time, Pallas kernels for 0%

commit v1 on v0

v1 whole, which is shorter than its diff:
```python
import functools

import jax
import jax.numpy as jnp
from jax import lax
from jax.experimental import pallas as pl
from jax.experimental.pallas import tpu as pltpu
from jax.sharding import PartitionSpec as P

MESH = pl.DeviceIdType.MESH
F32 = jnp.float32
BF16 = jnp.bfloat16

REACH = 4
BLOCKS = 2 * REACH + 1
CHUNKS = 2
PACKED = 272


def packed_rows(squares):
    row = lax.broadcasted_iota(jnp.int32, (64, 128), 0)
    lane = lax.broadcasted_iota(jnp.int32, (64, 128), 1)
    parts, diagonals = [], []
    for square in squares:
        low = pltpu.roll(square[64:], 64, 1)
        parts.append(jnp.where(lane < row, low, square[:64]))
        diagonals.append(jnp.sum(jnp.where(lane == row, low, 0.0), axis=0, keepdims=True))
    return parts, jnp.concatenate(diagonals + [jnp.zeros((12, 128), F32)], axis=0)


def unpacked(part, diagonal):
    row = lax.broadcasted_iota(jnp.int32, (64, 128), 0)
    lane = lax.broadcasted_iota(jnp.int32, (64, 128), 1)
    upper = jnp.where(lane > row, part, 0.0)
    lower = pltpu.roll(jnp.where(lane < row, part, 0.0), 64, 1)
    strict = jnp.concatenate([upper, lower], axis=0)
    first = jnp.where(lane == row, part, 0.0)
    second = jnp.where(lane == row + 64, pltpu.roll(jnp.broadcast_to(diagonal, (8, 128)), 64, 1)[:1], 0.0)
    return strict + strict.T + jnp.concatenate([first, second], axis=0)


def kernel(
    pairs_count,
    fac, coef, amp, dom, prt, cpl, eng,
    out,
    cw, tw, dw, fbuf, wide, slab_own, slab_out, slab_in, up_out, up_in, down_out, down_in, inter, mixed,
    own_sem, fac_sem,
    c_send, c_recv, t_send, t_recv, d_send, d_recv,
    cs_send, cs_recv, ts_send, ts_recv, ds_send, ds_recv,
    far_send, slab_send, slab_recv, up_send, up_recv, down_send, down_recv,
):
    aux = lax.axis_index("aux")
    me = lax.axis_index("pairs") * 16 + aux
    total = pairs_count * 16
    chip = me // 2
    chips = total // 2
    core = lax.rem(aux, 2)
    z = aux // 2
    other = me + 1 - 2 * core
    column = me - aux
    above = column + lax.rem(aux + 2, 16)
    below = column + lax.rem(aux + 14, 16)
    has_up = me + 2 < total
    has_down = me >= 2
    feeds_first = (chip > REACH) & (chip <= 2 * REACH)
    feeds_last = (chip >= chips - 1 - 2 * REACH) & (chip < chips - 1 - REACH)
    is_first = chip == 0
    is_last = chip == chips - 1
    goes = (has_up, has_down)

    def place(d):
        d = lax.rem(d + total, total)
        return {"pairs": d // 16, "aux": lax.rem(d, 16)}

    barrier = pltpu.get_barrier_semaphore()

    def greet(d):
        pl.semaphore_signal(barrier, inc=1, device_id=place(d), device_id_type=MESH)

    greet(other)
    greet(above)
    greet(below)

    @pl.when((z == 7) & has_up)
    def _():
        greet(me + 2)

    @pl.when((z == 0) & has_down)
    def _():
        greet(me - 2)

    @pl.when(feeds_first)
    def _():
        greet(core)

    @pl.when(feeds_last)
    def _():
        greet(total - 2 + core)

    @pl.when(is_first)
    def _():
        for s in range(1, REACH + 1):
            greet(2 * (2 * REACH + 1 - s) + core)

    @pl.when(is_last)
    def _():
        for s in range(1, REACH + 1):
            greet(2 * (chips - 2 - 2 * REACH + s) + core)

    one = lambda flag: flag.astype(jnp.int32)
    pl.semaphore_wait(
        barrier,
        3
        + one((z == 7) & has_up)
        + one((z == 0) & has_down)
        + one(feeds_first)
        + one(feeds_last)
        + REACH * (one(is_first) + one(is_last)),
    )

    def piece(k, slot, c):
        if k < CHUNKS:
            return cw.at[pl.ds(slot * 8 + c * 4 + k * 2, 2)]
        if k == CHUNKS:
            return tw.at[pl.ds(slot * 8 + c * 4, 4)]
        return dw.at[slot * 2 + c]

    def source(k):
        if k < CHUNKS:
            return coef.at[pl.ds(k * 2, 2)]
        if k == CHUNKS:
            return amp
        return dom

    sends = (c_send, c_send, t_send, d_send)
    recvs = (c_recv, c_recv, t_recv, d_recv)
    sib_sends = (cs_send, cs_send, ts_send, ds_send)
    sib_recvs = (cs_recv, cs_recv, ts_recv, ds_recv)
    C0, C1, T, D = 0, 1, 2, 3

    def at_slot(dr, s):
        return REACH - s if dr == 0 else REACH + s

    def ring(dr, s, k):
        src = source(k) if s == 1 else piece(k, at_slot(dr, s - 1), core)
        return pltpu.make_async_remote_copy(
            src, piece(k, at_slot(dr, s), core),
            sends[k].at[dr, s - 1, k % 2], recvs[k].at[dr, s - 1, k % 2],
            device_id=place(me + 2 if dr == 0 else me - 2), device_id_type=MESH,
        )

    def ring_start(dr, s, k):
        @pl.when(goes[dr])
        def _():
            ring(dr, s, k).start()

    def to_sibling(slot, k):
        src = source(k) if slot == REACH else piece(k, slot, core)
        return pltpu.make_async_remote_copy(
            src, piece(k, slot, core),
            sib_sends[k].at[slot, k % 2], sib_recvs[k].at[slot, k % 2],
            device_id=place(other), device_id_type=MESH,
        )

    def to_first(k):
        slot = chip - (REACH + 1)
        return pltpu.make_async_remote_copy(
            source(k), piece(k, slot, core),
            far_send.at[0, k], recvs[k].at[0, REACH - 1 - slot, k % 2],
            device_id=place(core), device_id_type=MESH,
        )

    def to_last(k):
        s = chip - (chips - 2 - 2 * REACH)
        return pltpu.make_async_remote_copy(
            source(k), piece(k, REACH + s, core),
            far_send.at[1, k], recvs[k].at[1, s - 1, k % 2],
            device_id=place(total - 2 + core), device_id_type=MESH,
        )

    def own(k):
        return pltpu.make_async_copy(source(k), piece(k, REACH, core), own_sem.at[k])

    def begin(k):
        for dr in range(2):
            ring_start(dr, 1, k)

        @pl.when(feeds_first)
        def _():
            to_first(k).start()

        @pl.when(feeds_last)
        def _():
            to_last(k).start()

    def arrive(dr, s, k):
        ring_recv(dr, s, k)
        if s < REACH:
            ring_start(dr, s + 1, k)
        to_sibling(at_slot(dr, s), k).start()

    def ring_recv(dr, s, k):
        ring(dr, s, k).wait_recv()

    def column_of(k):
        off = jnp.where(lax.rem(k, 2) == 0, 4 - k // 2, k // 2 - 3)
        return lax.rem(z + off + 8, 8)

    def fac_copy(k):
        return pltpu.make_async_copy(
            fac.at[:, pl.ds(pl.multiple_of(column_of(k) * 8, 8), 8), :], fbuf.at[k], fac_sem.at[k]
        )

    for k in (D, C0, C1):
        begin(k)
    for k in range(8):
        fac_copy(k).start()
    for k in (D, C0, C1, T):
        own(k).start()
        to_sibling(REACH, k).start()

    def slab_to_sibling(k):
        return pltpu.make_async_remote_copy(
            slab_out.at[k], slab_in.at[k], slab_send.at[k], slab_recv.at[k],
            device_id=place(other), device_id_type=MESH,
        )

    def slab_group(k, carry):
        fac_copy(k).wait()
        wide[...] = fbuf[k].astype(F32).reshape(2048, 128)
        squares = []
        for j in range(8):
            rows = wide[pl.ds(j, 256, stride=8), :].astype(BF16)
            squares.append(
                lax.dot_general(rows, rows, (((0,), (0,)), ((), ())), preferred_element_type=F32)
            )
        halves = [packed_rows(squares[:4]), packed_rows(squares[4:])]

        def put(ref, half):
            parts, diagonals = half
            for i, part in enumerate(parts):
                ref[k, pl.ds(i * 64, 64), :] = part.astype(BF16)
            ref[k, pl.ds(256, 16), :] = diagonals.astype(BF16)

        @pl.when(core == 0)
        def _():
            put(slab_own, halves[0])
            put(slab_out, halves[1])

        @pl.when(core == 1)
        def _():
            put(slab_own, halves[1])
            put(slab_out, halves[0])

        slab_to_sibling(k).start()
        return carry

    def chip_sum(k):
        slab_to_sibling(k).wait_recv()
        return slab_own[k].astype(F32) + slab_in[k].astype(F32)

    def up_copy(r):
        return pltpu.make_async_remote_copy(
            up_out.at[r], up_in.at[r], up_send.at[r], up_recv.at[r],
            device_id=place(above), device_id_type=MESH,
        )

    def down_copy(r):
        return pltpu.make_async_remote_copy(
            down_out.at[r], down_in.at[r], down_send.at[r], down_recv.at[r],
            device_id=place(below), device_id_type=MESH,
        )

    def sum_step(r):
        value = chip_sum(2 * r)
        if r > 0:
            up_copy(r - 1).wait_recv()
            value = value + up_in[r - 1].astype(F32)
        up_out[r] = value.astype(BF16)
        up_copy(r).start()
        if r < 3:
            value = chip_sum(2 * r + 1)
            if r > 0:
                down_copy(r - 1).wait_recv()
                value = value + down_in[r - 1].astype(F32)
            down_out[r] = value.astype(BF16)
            down_copy(r).start()

    lax.fori_loop(0, 4, slab_group, 0)
    for dr in range(2):
        arrive(dr, 1, D)
        arrive(dr, 1, C0)
    lax.fori_loop(4, 8, slab_group, 0)
    sum_step(0)
    for dr in range(2):
        arrive(dr, 1, C1)
    for s in range(2, REACH + 1):
        for dr in range(2):
            arrive(dr, s, D)
            arrive(dr, s, C0)
        sum_step(s - 1)
        if s == REACH:
            begin(T)
        for dr in range(2):
            arrive(dr, s, C1)

    up_copy(3).wait_recv()
    down_copy(2).wait_recv()
    summed = chip_sum(7) + up_in[3].astype(F32) + down_in[2].astype(F32)
    for j in range(4):
        out[j] = unpacked(summed[j * 64 : (j + 1) * 64], summed[256 + j : 257 + j])

    for k in (D, C0, C1):
        own(k).wait()
        for slot in range(BLOCKS):
            to_sibling(slot, k).wait_recv()

    def slot_of(q):
        apart = q // 8 - chip
        apart = jnp.where(apart > REACH, apart - BLOCKS, apart)
        apart = jnp.where(apart < -REACH, apart + BLOCKS, apart)
        return jnp.clip(apart + REACH, 0, BLOCKS - 1) * 8 + lax.rem(q, 8)

    def intersect(p):
        mine = cw[REACH * 8 + core * 4 + p]
        mine_t = mine.T
        rows = dw[REACH * 2 + core]
        funcs = jnp.broadcast_to(rows[p : p + 1], (128, 256)).T
        funcs = jnp.concatenate([funcs, funcs], axis=1)
        for c in range(12):
            slot = slot_of(prt[p, c])
            theirs = dw[slot // 4, pl.ds(lax.rem(slot, 4), 1), :]
            same = (funcs == theirs).astype(F32).astype(BF16)
            spread = jnp.dot(mine_t, same, preferred_element_type=F32).astype(BF16)
            inter[p, :, c * 128 : (c + 1) * 128] = jnp.dot(
                spread, cw[slot], preferred_element_type=F32
            ).astype(BF16)

    for p in range(4):
        intersect(p)
        for dr in range(2):
            arrive(dr, p + 1, T)

    own(T).wait()
    for slot in range(BLOCKS):
        to_sibling(slot, T).wait_recv()

    for p in range(4):
        for c in range(12):
            slot = slot_of(prt[p, c])
            part = jnp.dot(inter[p, :, c * 128 : (c + 1) * 128], tw[slot], preferred_element_type=F32)
            mixed[:, c * 128 : (c + 1) * 128] = (part * cpl[p, c]).astype(BF16)
        cycle = lax.dot_general(
            mixed[...], inter[p], (((1,), (1,)), ((), ())), preferred_element_type=F32
        )
        level = jnp.broadcast_to(eng[p : p + 1, :], (128, 128))
        own_amp = tw[REACH * 8 + core * 4 + p].astype(F32)
        out[p] = out[p] + (level + level.T) * own_amp - cycle

    for k in (D, C0, C1, T):
        for dr in range(2):
            @pl.when(goes[dr])
            def _():
                for s in range(1, REACH + 1):
                    ring(dr, s, k).wait_send()
        for slot in range(BLOCKS):
            to_sibling(slot, k).wait_send()

        @pl.when(feeds_first)
        def _():
            to_first(k).wait_send()

        @pl.when(feeds_last)
        def _():
            to_last(k).wait_send()

    for k in range(8):
        slab_to_sibling(k).wait_send()
    for r in range(4):
        up_copy(r).wait_send()
    for r in range(3):
        down_copy(r).wait_send()


def solution(mesh):
    pairs_count = mesh.shape["pairs"]
    dma = pltpu.SemaphoreType.DMA
    whole = pl.BlockSpec(memory_space=pltpu.VMEM)
    any_space = pl.BlockSpec(memory_space=pl.ANY)
    smem = pl.BlockSpec(memory_space=pltpu.SMEM)
    block = (PACKED, 128)
    call = pl.pallas_call(
        functools.partial(kernel, pairs_count),
        out_shape=jax.ShapeDtypeStruct((4, 128, 128), F32),
        in_specs=[any_space, any_space, any_space, any_space, smem, smem, whole],
        out_specs=whole,
        scratch_shapes=[
            pltpu.VMEM((BLOCKS * 8, 256, 128), BF16),
            pltpu.VMEM((BLOCKS * 8, 128, 128), BF16),
            pltpu.VMEM((BLOCKS * 2, 4, 256), jnp.int32),
            pltpu.VMEM((8, 256, 8, 128), BF16),
            pltpu.VMEM((2048, 128), F32),
            pltpu.VMEM((8,) + block, BF16),
            pltpu.VMEM((8,) + block, BF16),
            pltpu.VMEM((8,) + block, BF16),
            pltpu.VMEM((4,) + block, BF16),
            pltpu.VMEM((4,) + block, BF16),
            pltpu.VMEM((3,) + block, BF16),
            pltpu.VMEM((3,) + block, BF16),
            pltpu.VMEM((4, 128, 1536), BF16),
            pltpu.VMEM((128, 1536), BF16),
            dma((4,)),
            dma((8,)),
        ]
        + [dma((2, REACH, 2))] * 6
        + [dma((BLOCKS, 2))] * 6
        + [dma((2, 4)), dma((8,)), dma((8,)), dma((4,)), dma((4,)), dma((3,)), dma((3,))],
        compiler_params=pltpu.CompilerParams(
            collective_id=0, has_side_effects=True, vmem_limit_bytes=48 << 20
        ),
    )
    split = P(("pairs", "aux"), None)
    cube = P(("pairs", "aux"), None, None)
    return jax.shard_map(
        call,
        mesh=mesh,
        in_specs=(P("aux", "pairs", None), cube, cube, split, split, split, split),
        out_specs=cube,
        check_vma=False,
    )
```

time: 169 us -> 94.6 us (0.56)
  the two profiles are of different devices: /device:TPU:1 before, /device:TPU:63 now
where the time goes in v1:
time: 94.6 us; the launch traced here: 94.3 us
  Pallas kernels  86.8 us (92%)
  local copies, waits for them, and re-layouts  7.48 us (8%)
    pallas_call x1, Pallas kernels  86.8 us
    unnamed x15, local copies, waits for them, and re-layouts  7.48 us

profile of v1, /device:TPU:63, one launch (start us, length us, event | category | flops | bytes accessed | tf_op | source)
XLA Modules:
  0.0 94.3 jit_solution(3861541144985230224)
XLA Ops:
  0.0 0.0 copy-start
  0.0 2.2 %copy-done = bf16[256,64,128]{2,1,0:T(8,128)(2,1)S(1)} copy-done((bf16[256,64,128]{2,1,0:T(8,128)(2,1)S(1)}, bf16[256,64,128]{2,1,0:T(8,128)(2,1)}, u32[]{:S(2)}) %copy-start) | copy-done | bytes 4194328
  2.2 0.0 copy-start.1
  2.2 0.9 %copy-done.1 = bf16[4,256,128]{2,1,0:T(8,128)(2,1)S(1)} copy-done((bf16[4,256,128]{2,1,0:T(8,128)(2,1)S(1)}, bf16[4,256,128]{2,1,0:T(8,128)(2,1)}, u32[]{:S(2)}) %copy-start.1) | copy-done | bytes 262168
  3.1 0.0 copy-start.2
  3.1 0.9 copy-done.2
  4.0 0.0 copy-start.3
  4.0 0.7 copy-done.3
  4.7 0.0 copy-start.4
  4.7 0.7 copy-done.4
  5.4 0.0 copy-start.5
  5.4 0.7 copy-done.5
  6.1 0.0 copy-start.6
  6.1 0.7 copy-done.6
  6.8 86.8 %shard_map.73 = f32[4,128,128]{2,1,0:T(8,128)S(1)} custom-call(bf16[256,64,128]{2,1,0:T(8,128)(2,1)S(1)} %copy-done, bf16[4,256,128]{2,1,0:T(8,128)(2,1)S(1)} %copy-done.1, bf16[4,128,128]{2,1,0:T(8,128)(2,1)S(1)} %copy-done.2, s32[4,256]{1,0:T(4,128)S(1)} %copy-done.3, s32[4,12]{1,0:T(4,128)S(1)} %copy-done.4, f32[4,12]{1,0:T(4,128)S(1)} %copy-done.5, ...), custom_call_target="tpu_custom_call" | custom-call | tf_op jit(solution)/shard_map/pallas_call
  93.6 0.7 copy.9
Async XLA Ops:
  0.0 2.2 %copy-start = (bf16[256,64,128]{2,1,0:T(8,128)(2,1)S(1)}, bf16[256,64,128]{2,1,0:T(8,128)(2,1)}, u32[]{:S(2)}) copy-start(bf16[256,64,128]{2,1,0:T(8,128)(2,1)} %fac.1) | copy-start | bytes 12582916
  2.2 0.9 %copy-start.1 = (bf16[4,256,128]{2,1,0:T(8,128)(2,1)S(1)}, bf16[4,256,128]{2,1,0:T(8,128)(2,1)}, u32[]{:S(2)}) copy-start(bf16[4,256,128]{2,1,0:T(8,128)(2,1)} %coef.1) | copy-start | bytes 786436
  3.1 0.9 copy-start.2
  4.0 0.7 copy-start.3
  4.7 0.7 copy-start.4
  5.4 0.7 copy-start.5
  6.1 0.7 copy-start.6

commit v2 on v1

v2 whole, which is shorter than its diff:
```python
import functools

import jax
import jax.numpy as jnp
from jax import lax
from jax.experimental import pallas as pl
from jax.experimental.pallas import tpu as pltpu
from jax.sharding import PartitionSpec as P

MESH = pl.DeviceIdType.MESH
F32 = jnp.float32
BF16 = jnp.bfloat16

REACH = 4
BLOCKS = 2 * REACH + 1
PACKED = 272


def packed_rows(squares):
    row = lax.broadcasted_iota(jnp.int32, (64, 128), 0)
    lane = lax.broadcasted_iota(jnp.int32, (64, 128), 1)
    parts, diagonals = [], []
    for square in squares:
        low = pltpu.roll(square[64:], 64, 1)
        parts.append(jnp.where(lane < row, low, square[:64]))
        diagonals.append(jnp.sum(jnp.where(lane == row, low, 0.0), axis=0, keepdims=True))
    return parts, jnp.concatenate(diagonals + [jnp.zeros((12, 128), F32)], axis=0)


def unpacked(part, diagonal):
    row = lax.broadcasted_iota(jnp.int32, (64, 128), 0)
    lane = lax.broadcasted_iota(jnp.int32, (64, 128), 1)
    upper = jnp.where(lane > row, part, 0.0)
    lower = pltpu.roll(jnp.where(lane < row, part, 0.0), 64, 1)
    strict = jnp.concatenate([upper, lower], axis=0)
    first = jnp.where(lane == row, part, 0.0)
    second = jnp.where(lane == row + 64, pltpu.roll(jnp.broadcast_to(diagonal, (8, 128)), 64, 1)[:1], 0.0)
    return strict + strict.T + jnp.concatenate([first, second], axis=0)


def kernel(
    pairs_count,
    fac, coef, amp, dom, prt_hbm, cpl_hbm, eng_hbm,
    out,
    cw, tw, dw, prt, cpl, eng, fbuf, wide, slab_own, slab_out, slab_in, up_out, up_in, down_out, down_in, inter, mixed,
    own_sem, fac_sem, small_sem,
    ring_send, ring_recv, sib_send, sib_recv, far_send,
    slab_send, slab_recv, up_send, up_recv, down_send, down_recv,
):
    aux = lax.axis_index("aux")
    me = lax.axis_index("pairs") * 16 + aux
    total = pairs_count * 16
    chip = me // 2
    chips = total // 2
    core = lax.rem(aux, 2)
    z = aux // 2
    other = me + 1 - 2 * core
    column = me - aux
    above = column + lax.rem(aux + 2, 16)
    below = column + lax.rem(aux + 14, 16)
    goes = (me + 2 < total, me >= 2)
    reach = (me + 2, me - 2)
    feeds = (chip == 2 * REACH, chip == chips - 1 - 2 * REACH)
    ends = (core, total - 2 + core)
    is_end = (chip == 0, chip == chips - 1)
    feeders = (4 * REACH + core, total - 2 - 4 * REACH + core)

    def place(d):
        d = lax.rem(d + total, total)
        return {"pairs": d // 16, "aux": lax.rem(d, 16)}

    barrier = pltpu.get_barrier_semaphore()
    greeted = jnp.int32(0)
    for flag, d in (
        (None, other), (None, above), (None, below),
        ((z == 7) & goes[0], reach[0]), ((z == 0) & goes[1], reach[1]),
        (feeds[0], ends[0]), (feeds[1], ends[1]), (is_end[0], feeders[0]), (is_end[1], feeders[1]),
    ):
        def greet(d=d):
            pl.semaphore_signal(barrier, inc=1, device_id=place(d), device_id_type=MESH)

        if flag is None:
            greet()
            greeted = greeted + 1
        else:
            pl.when(flag)(greet)
            greeted = greeted + flag.astype(jnp.int32)
    pl.semaphore_wait(barrier, greeted)

    def piece(kind, k, slot, c):
        if kind == "C":
            return cw.at[slot * 8 + c * 4 + k]
        if kind == "T":
            return tw.at[pl.ds(slot * 8 + c * 4 + k * 2, 2)]
        return dw.at[slot * 2 + c]

    def source(kind, k):
        if kind == "C":
            return coef.at[k]
        if kind == "T":
            return amp.at[pl.ds(k * 2, 2)]
        return dom

    def mark(kind, k):
        return k + {"C": 0, "T": 4, "D": 6}[kind]

    def at_slot(dr, s):
        return REACH - s if dr == 0 else REACH + s

    def hop(dr, s, kind, k, first, to, send_sem):
        src = source(kind, k) if first else piece(kind, k, at_slot(dr, s - 1), core)
        return pltpu.make_async_remote_copy(
            src, piece(kind, k, at_slot(dr, s), core), send_sem, ring_recv.at[dr, s - 1, mark(kind, k)],
            device_id=place(to), device_id_type=MESH,
        )

    def ring(dr, s, kind, k, first=False):
        return hop(dr, s, kind, k, first, reach[dr], ring_send.at[dr, s - 1, mark(kind, k)])

    def far(dr, s, kind, k, first=False):
        return hop(dr, s, kind, k, first, ends[dr], far_send.at[s - 1, mark(kind, k)])

    def pass_on(dr, s, kind, k, first=False):
        @pl.when(goes[dr])
        def _():
            ring(dr, s, kind, k, first).start()

        @pl.when(feeds[dr])
        def _():
            far(dr, s, kind, k, first).start()

    def to_sibling(slot, kind, k, first=False):
        src = source(kind, k) if first else piece(kind, k, slot, core)
        m = mark(kind, k)
        return pltpu.make_async_remote_copy(
            src, piece(kind, k, slot, core), sib_send.at[slot, m], sib_recv.at[slot, m],
            device_id=place(other), device_id_type=MESH,
        )

    def own(kind, k):
        return pltpu.make_async_copy(source(kind, k), piece(kind, k, REACH, core), own_sem.at[mark(kind, k)])

    def begin(kind, k):
        for dr in range(2):
            pass_on(dr, 1, kind, k, True)

    def arrive(s, kind, k, last=False):
        for dr in range(2):
            ring(dr, s, kind, k).wait_recv()
            if not last:
                pass_on(dr, s + 1, kind, k)
            to_sibling(at_slot(dr, s), kind, k).start()

    pieces = [("D", 0)] + [("C", k) for k in range(4)] + [("T", k) for k in range(2)]

    def column_of(k):
        off = jnp.where(lax.rem(k, 2) == 0, 4 - k // 2, k // 2 - 3)
        return lax.rem(z + off + 8, 8)

    def fac_copy(k):
        return pltpu.make_async_copy(
            fac.at[:, pl.ds(pl.multiple_of(column_of(k) * 8, 8), 8), :], fbuf.at[k], fac_sem.at[k]
        )

    smalls = [
        pltpu.make_async_copy(src, dst, small_sem.at[i])
        for i, (src, dst) in enumerate(((prt_hbm, prt), (cpl_hbm, cpl), (eng_hbm, eng)))
    ]

    for kind, k in pieces[:5]:
        begin(kind, k)
    lax.fori_loop(0, 8, lambda k, carry: (fac_copy(k).start(), carry)[1], 0)
    for kind, k in pieces:
        own(kind, k).start()
        to_sibling(REACH, kind, k, True).start()
    for copy in smalls:
        copy.start()

    def slab_to_sibling(k):
        return pltpu.make_async_remote_copy(
            slab_out.at[k], slab_in.at[k], slab_send.at[k], slab_recv.at[k],
            device_id=place(other), device_id_type=MESH,
        )

    def slab_group(k):
        fac_copy(k).wait()
        wide[...] = fbuf[k].astype(F32).reshape(2048, 128)
        squares = []
        for j in range(8):
            rows = wide[pl.ds(j, 256, stride=8), :].astype(BF16)
            squares.append(
                lax.dot_general(rows, rows, (((0,), (0,)), ((), ())), preferred_element_type=F32)
            )
        halves = [packed_rows(squares[:4]), packed_rows(squares[4:])]

        def put(ref, half):
            parts, diagonals = half
            for i, part in enumerate(parts):
                ref[k, pl.ds(i * 64, 64), :] = part.astype(BF16)
            ref[k, pl.ds(256, 16), :] = diagonals.astype(BF16)

        @pl.when(core == 0)
        def _():
            put(slab_own, halves[0])
            put(slab_out, halves[1])

        @pl.when(core == 1)
        def _():
            put(slab_own, halves[1])
            put(slab_out, halves[0])

        slab_to_sibling(k).start()

    def chip_sum(k):
        slab_to_sibling(k).wait_recv()
        return slab_own[k].astype(F32) + slab_in[k].astype(F32)

    def up_copy(r):
        return pltpu.make_async_remote_copy(
            up_out.at[r], up_in.at[r], up_send.at[r], up_recv.at[r],
            device_id=place(above), device_id_type=MESH,
        )

    def down_copy(r):
        return pltpu.make_async_remote_copy(
            down_out.at[r], down_in.at[r], down_send.at[r], down_recv.at[r],
            device_id=place(below), device_id_type=MESH,
        )

    def sum_step(r):
        value = chip_sum(2 * r)
        if r > 0:
            up_copy(r - 1).wait_recv()
            value = value + up_in[r - 1].astype(F32)
        up_out[r] = value.astype(BF16)
        up_copy(r).start()
        if r < 3:
            value = chip_sum(2 * r + 1)
            if r > 0:
                down_copy(r - 1).wait_recv()
                value = value + down_in[r - 1].astype(F32)
            down_out[r] = value.astype(BF16)
            down_copy(r).start()

    def loop(low, high):
        def run(body):
            def step(i, carry):
                body(i)
                return carry

            lax.fori_loop(low, high, step, 0)

        return run

    @loop(0, 4)
    def _(i):
        slab_group(i)
        arrive(1, "C", i)

    arrive(1, "D", 0)
    for k in range(2):
        begin("T", k)
    @loop(0, 4)
    def _(i):
        slab_group(4 + i)
        arrive(2, "C", i)

    arrive(2, "D", 0)
    for k in range(2):
        arrive(1, "T", k)
    sum_step(0)

    @loop(0, 4)
    def _(i):
        arrive(3, "C", i)

    arrive(3, "D", 0)
    for k in range(2):
        arrive(2, "T", k)
    sum_step(1)

    @loop(0, 4)
    def _(i):
        arrive(4, "C", i, True)

    arrive(4, "D", 0, True)
    sum_step(2)

    for copy in smalls:
        copy.wait()
    for kind, k in pieces[:5]:
        own(kind, k).wait()

    @loop(0, BLOCKS)
    def _(slot):
        for kind, k in pieces[:5]:
            to_sibling(slot, kind, k).wait_recv()

    def slot_of(q):
        apart = q // 8 - chip
        apart = jnp.where(apart > REACH, apart - BLOCKS, apart)
        apart = jnp.where(apart < -REACH, apart + BLOCKS, apart)
        return jnp.clip(apart + REACH, 0, BLOCKS - 1) * 8 + lax.rem(q, 8)

    def intersect(p):
        mine_t = cw[REACH * 8 + core * 4 + p].T
        funcs = jnp.broadcast_to(dw[REACH * 2 + core, pl.ds(p, 1), :], (128, 256)).T
        funcs = jnp.concatenate([funcs, funcs], axis=1)
        for c in range(12):
            slot = slot_of(prt[p, c])
            theirs = dw[slot // 4, pl.ds(lax.rem(slot, 4), 1), :]
            same = (funcs == theirs).astype(F32).astype(BF16)
            spread = jnp.dot(mine_t, same, preferred_element_type=F32).astype(BF16)
            inter[p, :, c * 128 : (c + 1) * 128] = jnp.dot(
                spread, cw[slot], preferred_element_type=F32
            ).astype(BF16)

    @loop(0, 2)
    def _(i):
        intersect(i)
        arrive(3, "T", i)

    @loop(0, 2)
    def _(i):
        intersect(2 + i)
        arrive(4, "T", i, True)

    sum_step(3)
    for k in range(2):
        own("T", k).wait()

    @loop(0, BLOCKS)
    def _(slot):
        for kind, k in pieces[5:]:
            to_sibling(slot, kind, k).wait_recv()

    for p in range(4):
        for c in range(12):
            slot = slot_of(prt[p, c])
            part = jnp.dot(inter[p, :, c * 128 : (c + 1) * 128], tw[slot], preferred_element_type=F32)
            mixed[:, c * 128 : (c + 1) * 128] = (part * cpl[p, c]).astype(BF16)
        cycle = lax.dot_general(
            mixed[...], inter[p], (((1,), (1,)), ((), ())), preferred_element_type=F32
        )
        level = jnp.broadcast_to(eng[p : p + 1, :], (128, 128))
        own_amp = tw[REACH * 8 + core * 4 + p].astype(F32)
        out[p] = (level + level.T) * own_amp - cycle

    up_copy(3).wait_recv()
    down_copy(2).wait_recv()
    summed = chip_sum(7) + up_in[3].astype(F32) + down_in[2].astype(F32)
    for p in range(4):
        out[p] = out[p] + unpacked(summed[p * 64 : (p + 1) * 64], summed[256 + p : 257 + p])


    for dr in range(2):
        for test, copy in ((goes[dr], ring), (feeds[dr], far)):
            @pl.when(test)
            def _():
                @loop(1, REACH + 1)
                def _(s):
                    for kind, k in pieces:
                        copy(dr, s, kind, k).wait_send()

    @loop(0, BLOCKS)
    def _(slot):
        for kind, k in pieces:
            to_sibling(slot, kind, k).wait_send()

    for k in range(8):
        slab_to_sibling(k).wait_send()
    for r in range(4):
        up_copy(r).wait_send()
    for r in range(3):
        down_copy(r).wait_send()


def solution(mesh):
    pairs_count = mesh.shape["pairs"]
    dma = pltpu.SemaphoreType.DMA
    whole = pl.BlockSpec(memory_space=pltpu.VMEM)
    hbm = pl.BlockSpec(memory_space=pltpu.HBM)
    block = (PACKED, 128)
    call = pl.pallas_call(
        functools.partial(kernel, pairs_count),
        out_shape=jax.ShapeDtypeStruct((4, 128, 128), F32),
        in_specs=[hbm] * 7,
        out_specs=whole,
        scratch_shapes=[
            pltpu.VMEM((BLOCKS * 8, 256, 128), BF16),
            pltpu.VMEM((BLOCKS * 8, 128, 128), BF16),
            pltpu.VMEM((BLOCKS * 2, 4, 256), jnp.int32),
            pltpu.SMEM((4, 12), jnp.int32),
            pltpu.SMEM((4, 12), F32),
            pltpu.VMEM((4, 128), F32),
            pltpu.VMEM((8, 256, 8, 128), BF16),
            pltpu.VMEM((2048, 128), F32),
            pltpu.VMEM((8,) + block, BF16),
            pltpu.VMEM((8,) + block, BF16),
            pltpu.VMEM((8,) + block, BF16),
            pltpu.VMEM((4,) + block, BF16),
            pltpu.VMEM((4,) + block, BF16),
            pltpu.VMEM((3,) + block, BF16),
            pltpu.VMEM((3,) + block, BF16),
            pltpu.VMEM((4, 128, 1536), BF16),
            pltpu.VMEM((128, 1536), BF16),
            dma((7,)),
            dma((8,)),
            dma((3,)),
            dma((2, REACH, 7)),
            dma((2, REACH, 7)),
            dma((BLOCKS, 7)),
            dma((BLOCKS, 7)),
            dma((REACH, 7)),
            dma((8,)),
            dma((8,)),
            dma((4,)),
            dma((4,)),
            dma((3,)),
            dma((3,)),
        ],
        compiler_params=pltpu.CompilerParams(
            collective_id=0, has_side_effects=True, vmem_limit_bytes=58 << 20
        ),
    )
    split = P(("pairs", "aux"), None)
    cube = P(("pairs", "aux"), None, None)
    return jax.shard_map(
        call,
        mesh=mesh,
        in_specs=(P("aux", "pairs", None), cube, cube, split, split, split, split),
        out_specs=cube,
        check_vma=False,
    )
```

time: 94.6 us -> 68.4 us (0.72)
  the two profiles are of different devices: /device:TPU:63 before, /device:TPU:41 now
where the time goes in v2:
time: 68.4 us; the launch traced here: 68.3 us
  Pallas kernels  66.6 us (97%)
  local copies, waits for them, and re-layouts  1.67 us (2%)
    pallas_call x1, Pallas kernels  66.6 us
    unnamed x1, local copies, waits for them, and re-layouts  1.67 us

profile of v2, /device:TPU:41, one launch (start us, length us, event | category | flops | bytes accessed | tf_op | source)
XLA Modules:
  0.0 68.3 jit_solution(14625428663805477325)
XLA Ops:
  0.0 66.6 %shard_map.73 = f32[4,128,128]{2,1,0:T(8,128)} custom-call(bf16[256,64,128]{2,1,0:T(8,128)(2,1)} %fac.1, bf16[4,256,128]{2,1,0:T(8,128)(2,1)} %coef.1, bf16[4,128,128]{2,1,0:T(8,128)(2,1)} %amp.1, s32[4,256]{1,0:T(4,128)} %dom.1, s32[4,12]{1,0:T(4,128)} %prt_hbm.1, f32[4,12]{1,0:T(4,128)} %cpl_hbm.1, f32[4,128]{1,0:T(4,128)} %eng_hbm.1), custom_call_target="tpu_custom_call" | custom-call | tf_op jit(solution)/shard_map/pallas_call
  66.6 1.7 %copy.9 = f32[4,128,128]{2,1,0:T(8,128)} copy(f32[4,128,128]{2,1,0:T(8,128)} %shard_map.73) | data formatting | bytes 524288

commit v3 on v2

--- a/solution.py
+++ b/solution.py
@@ -215,32 +215,37 @@
         slab_to_sibling(k).wait_recv()
         return slab_own[k].astype(F32) + slab_in[k].astype(F32)
 
-    def up_copy(r):
+    halves_of = (pl.ds(0, 144), pl.ds(144, 128))
+    stage_blocks = ((0, 2, 4, 6), (0, 1, 3, 5))
+
+    def sum_copy(dr, r):
+        outgoing, incoming, send, recv, to = (
+            (up_out, up_in, up_send, up_recv, above),
+            (down_out, down_in, down_send, down_recv, below),
+        )[dr]
+        rows = halves_of[dr] if r == 0 else pl.ds(0, PACKED)
         return pltpu.make_async_remote_copy(
-            up_out.at[r], up_in.at[r], up_send.at[r], up_recv.at[r],
-            device_id=place(above), device_id_type=MESH,
-        )
-
-    def down_copy(r):
-        return pltpu.make_async_remote_copy(
-            down_out.at[r], down_in.at[r], down_send.at[r], down_recv.at[r],
-            device_id=place(below), device_id_type=MESH,
+            outgoing.at[r, rows], incoming.at[r, rows], send.at[r], recv.at[r],
+            device_id=place(to), device_id_type=MESH,
         )
 
     def sum_step(r):
-        value = chip_sum(2 * r)
-        if r > 0:
-            up_copy(r - 1).wait_recv()
-            value = value + up_in[r - 1].astype(F32)
-        up_out[r] = value.astype(BF16)
-        up_copy(r).start()
-        if r < 3:
-            value = chip_sum(2 * r + 1)
-            if r > 0:
-                down_copy(r - 1).wait_recv()
-                value = value + down_in[r - 1].astype(F32)
-            down_out[r] = value.astype(BF16)
-            down_copy(r).start()
+        opposite = chip_sum(0) if r == 0 else None
+        for dr, outgoing, incoming in ((0, up_out, up_in), (1, down_out, down_in)):
+            if r == 0:
+                rows = halves_of[dr]
+                outgoing[0, rows, :] = opposite[rows.start : rows.start + rows.size].astype(BF16)
+            else:
+                value = chip_sum(stage_blocks[dr][r])
+                sum_copy(dr, r - 1).wait_recv()
+                if r > 1:
+                    outgoing[r] = (value + incoming[r - 1].astype(F32)).astype(BF16)
+                else:
+                    rows, rest = halves_of[dr], halves_of[1 - dr]
+                    met = value[rows.start : rows.start + rows.size] + incoming[0, rows, :].astype(F32)
+                    outgoing[1, rows, :] = met.astype(BF16)
+                    outgoing[1, rest, :] = value[rest.start : rest.start + rest.size].astype(BF16)
+            sum_copy(dr, r).start()
 
     def loop(low, high):
         def run(body):
@@ -320,12 +325,13 @@
         intersect(i)
         arrive(3, "T", i)
 
+    sum_step(3)
+
     @loop(0, 2)
     def _(i):
         intersect(2 + i)
         arrive(4, "T", i, True)
 
-    sum_step(3)
     for k in range(2):
         own("T", k).wait()
 
@@ -346,9 +352,9 @@
         own_amp = tw[REACH * 8 + core * 4 + p].astype(F32)
         out[p] = (level + level.T) * own_amp - cycle
 
-    up_copy(3).wait_recv()
-    down_copy(2).wait_recv()
-    summed = chip_sum(7) + up_in[3].astype(F32) + down_in[2].astype(F32)
+    for dr in range(2):
+        sum_copy(dr, 3).wait_recv()
+    summed = chip_sum(7) + up_in[3].astype(F32) + down_in[3].astype(F32)
     for p in range(4):
         out[p] = out[p] + unpacked(summed[p * 64 : (p + 1) * 64], summed[256 + p : 257 + p])
 
@@ -370,9 +376,8 @@
     for k in range(8):
         slab_to_sibling(k).wait_send()
     for r in range(4):
-        up_copy(r).wait_send()
-    for r in range(3):
-        down_copy(r).wait_send()
+        for dr in range(2):
+            sum_copy(dr, r).wait_send()
 
 
 def solution(mesh):
@@ -400,8 +405,8 @@
             pltpu.VMEM((8,) + block, BF16),
             pltpu.VMEM((4,) + block, BF16),
             pltpu.VMEM((4,) + block, BF16),
-            pltpu.VMEM((3,) + block, BF16),
-            pltpu.VMEM((3,) + block, BF16),
+            pltpu.VMEM((4,) + block, BF16),
+            pltpu.VMEM((4,) + block, BF16),
             pltpu.VMEM((4, 128, 1536), BF16),
             pltpu.VMEM((128, 1536), BF16),
             dma((7,)),
@@ -416,8 +421,8 @@
             dma((8,)),
             dma((4,)),
             dma((4,)),
-            dma((3,)),
-            dma((3,)),
+            dma((4,)),
+            dma((4,)),
         ],
         compiler_params=pltpu.CompilerParams(
             collective_id=0, has_side_effects=True, vmem_limit_bytes=58 << 20

time: 68.4 us -> 67.7 us (0.990)
  Pallas kernels: 66.6 us -> 65.9 us
    pallas_call x1, Pallas kernels: 66.6 us -> 65.9 us
where the time goes in v3:
time: 67.7 us; the launch traced here: 67.6 us
  Pallas kernels  65.9 us (97%)
  local copies, waits for them, and re-layouts  1.67 us (2%)
    pallas_call x1, Pallas kernels  65.9 us
    unnamed x1, local copies, waits for them, and re-layouts  1.67 us

profile of v3, /device:TPU:41, one launch (start us, length us, event | category | flops | bytes accessed | tf_op | source)
XLA Modules:
  0.0 67.6 jit_solution(17697453231637739274)
XLA Ops:
  0.0 65.9 %shard_map.73 = f32[4,128,128]{2,1,0:T(8,128)} custom-call(bf16[256,64,128]{2,1,0:T(8,128)(2,1)} %fac.1, bf16[4,256,128]{2,1,0:T(8,128)(2,1)} %coef.1, bf16[4,128,128]{2,1,0:T(8,128)(2,1)} %amp.1, s32[4,256]{1,0:T(4,128)} %dom.1, s32[4,12]{1,0:T(4,128)} %prt_hbm.1, f32[4,12]{1,0:T(4,128)} %cpl_hbm.1, f32[4,128]{1,0:T(4,128)} %eng_hbm.1), custom_call_target="tpu_custom_call" | custom-call | tf_op jit(solution)/shard_map/pallas_call
  65.9 1.7 %copy.9 = f32[4,128,128]{2,1,0:T(8,128)} copy(f32[4,128,128]{2,1,0:T(8,128)} %shard_map.73) | data formatting | bytes 524288

commit v4 on v3

--- a/solution.py
+++ b/solution.py
@@ -325,12 +325,11 @@
         intersect(i)
         arrive(3, "T", i)
 
+    intersect(2)
+    arrive(4, "T", 0, True)
     sum_step(3)
-
-    @loop(0, 2)
-    def _(i):
-        intersect(2 + i)
-        arrive(4, "T", i, True)
+    intersect(3)
+    arrive(4, "T", 1, True)
 
     for k in range(2):
         own("T", k).wait()

time: 67.7 us -> 67.6 us (level)
  no operation moved by 1% of the time
where the time goes in v4:
time: 67.6 us; the launch traced here: 67.4 us
  Pallas kernels  65.8 us (97%)
  local copies, waits for them, and re-layouts  1.67 us (2%)
    pallas_call x1, Pallas kernels  65.8 us
    unnamed x1, local copies, waits for them, and re-layouts  1.67 us

profile of v4, /device:TPU:41, one launch (start us, length us, event | category | flops | bytes accessed | tf_op | source)
XLA Modules:
  0.0 67.4 jit_solution(2103593360688647770)
XLA Ops:
  0.0 65.8 %shard_map.73 = f32[4,128,128]{2,1,0:T(8,128)} custom-call(bf16[256,64,128]{2,1,0:T(8,128)(2,1)} %fac.1, bf16[4,256,128]{2,1,0:T(8,128)(2,1)} %coef.1, bf16[4,128,128]{2,1,0:T(8,128)(2,1)} %amp.1, s32[4,256]{1,0:T(4,128)} %dom.1, s32[4,12]{1,0:T(4,128)} %prt_hbm.1, f32[4,12]{1,0:T(4,128)} %cpl_hbm.1, f32[4,128]{1,0:T(4,128)} %eng_hbm.1), custom_call_target="tpu_custom_call" | custom-call | tf_op jit(solution)/shard_map/pallas_call
  65.8 1.7 %copy.9 = f32[4,128,128]{2,1,0:T(8,128)} copy(f32[4,128,128]{2,1,0:T(8,128)} %shard_map.73) | data formatting | bytes 524288
